TPU v7x, 32 devices: a whole 2x2x4 slice. The times are simulated.
32 devices in a mesh: dp: 4 (over y, x), expert: 8 (over z, core).
Axes of the slice: x: 2, y: 2, z: 4, core: 2. Of those that a mesh axis runs over, the one named last changes fastest.
Arguments:
- tokens: bfloat16 [512, 3584], P(('dp', 'expert')), may hold values from -6 to 6
- out_grad: bfloat16 [512, 3584], P(('dp', 'expert')), may hold values from -6 to 6
- route_ids: int32 [512, 8], P(('dp', 'expert')), may hold values from 0 to 15, all different within a row; in each aligned block of 16 rows (0 to 15, 16 to 31, ...) at most 16 rows name the same one
- route_probs: float32 [512, 8], P(('dp', 'expert')), may hold values from 0.02 to 0.5
- w_gate: bfloat16 [16, 3584, 1024], P('expert', None, 'dp'), may hold values from -0.09375 to 0.09375
- w_up: bfloat16 [16, 3584, 1024], P('expert', None, 'dp'), may hold values from -0.09375 to 0.09375
- w_down: bfloat16 [16, 1024, 3584], P('expert', 'dp'), may hold values from -0.1875 to 0.1875
Outputs:
- in_grad: bfloat16 [512, 3584], P(('dp', 'expert'))
Inputs may be any that keep to these rules, and one draw needn't show every extreme that they name: `route_ids`: the 8 ids of a token differ. Among the tokens of one device (aligned blocks of 16 rows) no expert is named more than 16 times, and in every draw some expert is named exactly 16 times there.
All inputs are finite; a program needn't handle non-finite values.
Results may differ from a plain program's by a relative error of at most 0.015.
Values may be sent and summed in bfloat16 or wider, within the bound.
A program may use at most 128 MiB of HBM per device.

v0:
```python
import jax
import jax.numpy as jnp
from jax import lax
from jax.sharding import PartitionSpec as P

TOPK = 8


def slot_matches(flat_ids, experts, capacity):
    onehot = (flat_ids[:, None] == jnp.arange(experts, dtype=jnp.int32)[None, :]).astype(jnp.int32)
    earlier = jnp.cumsum(onehot, axis=0) - onehot
    slot_rank = jnp.sum(earlier * onehot, axis=1)
    slot_of = flat_ids * capacity + slot_rank
    return slot_of[None, :] == jnp.arange(experts * capacity, dtype=jnp.int32)[:, None]


def select_matrix(matches, tok_count):
    return jnp.sum(matches.reshape(matches.shape[0], tok_count, TOPK).astype(jnp.float32), axis=2)


def build_tiles(token_rows, grad_rows, matches, flat_probs):
    select = select_matrix(matches, token_rows.shape[0]).astype(jnp.bfloat16)
    slot_scale = jnp.sum(jnp.where(matches, flat_probs[None, :], 0.0), axis=1)
    x_rows = jnp.dot(select, token_rows, preferred_element_type=jnp.float32).astype(jnp.bfloat16)
    g_rows = (
        jnp.dot(select, grad_rows, preferred_element_type=jnp.float32) * slot_scale[:, None]
    ).astype(jnp.bfloat16)
    return jnp.stack([x_rows, g_rows])


def expert_grads(tiles, w_gate, w_up, w_down):
    x_rows = tiles[:, 0]
    g_rows = tiles[:, 1]
    gate_pre = jnp.einsum("nsecd,edh->nsech", x_rows, w_gate, preferred_element_type=jnp.float32)
    up_pre = jnp.einsum("nsecd,edh->nsech", x_rows, w_up, preferred_element_type=jnp.float32)
    hidden_grad = jnp.einsum("nsecd,ehd->nsech", g_rows, w_down, preferred_element_type=jnp.float32)
    sigmoid_a = jax.nn.sigmoid(gate_pre)
    gate_grad = (hidden_grad * up_pre * sigmoid_a * (1.0 + gate_pre * (1.0 - sigmoid_a))).astype(
        jnp.bfloat16
    )
    up_grad = (hidden_grad * gate_pre * sigmoid_a).astype(jnp.bfloat16)
    partial_value = jnp.einsum(
        "nsech,edh->nsecd", gate_grad, w_gate, preferred_element_type=jnp.float32
    )
    partial_value = partial_value + jnp.einsum(
        "nsech,edh->nsecd", up_grad, w_up, preferred_element_type=jnp.float32
    )
    return partial_value.astype(jnp.bfloat16)


def on_device(tokens, out_grad, route_ids, route_probs, w_gate, w_up, w_down):
    columns = lax.axis_size("expert")
    local_experts = w_gate.shape[0]
    experts = local_experts * columns
    tok_count, width = tokens.shape
    capacity = max(2, 2 * tok_count * TOPK // experts)
    slots = experts * capacity
    tile_shape = (2, columns, local_experts, capacity, width)
    own_matches = slot_matches(route_ids.reshape(-1), experts, capacity)
    tiles = build_tiles(tokens, out_grad, own_matches, route_probs.reshape(-1)).reshape(
        (1,) + tile_shape
    )
    received = lax.all_to_all(tiles, "expert", split_axis=2, concat_axis=2, tiled=True)
    partials = expert_grads(
        lax.all_gather(received, "dp", axis=0, tiled=True), w_gate, w_up, w_down
    )
    summed = lax.psum_scatter(
        partials.astype(jnp.float32).astype(jnp.bfloat16), "dp", scatter_dimension=0, tiled=True
    ).astype(jnp.float32)
    returned = lax.all_to_all(
        summed.astype(jnp.bfloat16), "expert", split_axis=1, concat_axis=1, tiled=True
    ).astype(summed.dtype)
    own_select = select_matrix(own_matches, tok_count)
    result = jnp.dot(own_select.T, returned.reshape(slots, width), precision=lax.Precision.HIGHEST)
    return result.astype(jnp.bfloat16)


def solution(mesh):
    placed = (
        P(("dp", "expert"), None),
        P(("dp", "expert"), None),
        P(("dp", "expert"), None),
        P(("dp", "expert"), None),
        P("expert", None, "dp"),
        P("expert", None, "dp"),
        P("expert", "dp", None),
    )
    return jax.shard_map(
        on_device, mesh=mesh, in_specs=placed, out_specs=P(("dp", "expert"), None), check_vma=False
    )
```

profile of v0, /device:TPU:0, one launch (start us, length us, event | category | flops | bytes accessed | tf_op | source)
XLA Modules:
  0.0 492.9 jit_solution(5754461328527843374)
XLA Ops:
  6.5 0.8 copy.26
  7.5 0.2 reduce_window_sum.11
  7.7 0.2 select_reduce_fusion.1
  8.1 0.8 copy.28
  8.9 0.1 select_reduce_fusion
  9.1 0.7 convolution_convert_fusion
  9.7 1.6 fusion.4
  11.3 0.3 pad_maximum_fusion
  11.6 88.9 %all_to_all.10 = bf16[1,2,8,2,16,3584]{5,4,0,3,1,2:T(8,128)(2,1)S(1)} all-to-all(bf16[1,2,8,2,16,3584]{5,4,0,3,1,2:T(8,128)(2,1)S(1)} %pad_maximum_fusion), channel_id=1, replica_groups=mesh['dp'=4,'expert'=8] {'expert'}, dimensions={2} | all-to-all | bytes 7340032 | tf_op jit(solution)/shard_map/all_to_all | solution.py:63
  100.6 2.0 copy.31
  102.7 138.9 %all-gather.2.cloned.1.call-done = bf16[4,2,8,2,16,3584]{5,4,2,0,3,1:T(8,128)(2,1)} async-done(((bf16[1,2,8,2,16,3584]{5,4,2,0,3,1:T(8,128)(2,1)}), bf16[4,2,8,2,16,3584]{5,4,2,0,3,1:T(8,128)(2,1)}) %all-gather.2.cloned.1.call-update) | async-done | bytes 14680080 | tf_op jit(solution)/shard_map/all_gather | solution.py:65
  241.6 6.3 %fusion.14 = f32[4,8,2,16,256]{4,3,1,0,2:T(8,128)S(1)} fusion(bf16[2,3584,256]{2,1,0:T(8,128)(2,1)} %param.11, bf16[4,2,8,2,16,3584]{5,4,2,0,3,1:T(8,128)(2,1)} %all-gather.2.cloned.1.call-done), kind=kOutput, calls=%fused_computation.19 | convolution fusion | flops 1879048192 | bytes 12058624 | tf_op jit(solution)/shard_map/nsecd,edh->nsech/dot_general | solution.py:34
  248.0 2.0 copy-done.4
  249.9 4.3 fusion.17
  254.2 5.5 %fusion.29 = bf16[4,8,2,16,256]{4,3,1,0,2:T(8,128)(2,1)S(1)} fusion(f32[4,8,2,16,256]{4,3,1,0,2:T(8,128)S(1)} %fusion.17, bf16[2,3584,256]{2,1,0:T(8,128)(2,1)S(1)} %copy-done.3, bf16[4,2,8,2,16,3584]{5,4,2,0,3,1:T(8,128)(2,1)} %all-gather.2.cloned.1.call-done, f32[4,8,2,16,256]{4,3,1,0,2:T(8,128)S(1)} %fusion.14), kind=kOutput, calls=%fused_computation.24 | convolution fusion | flops 1881669632 | bytes 13631488 | tf_op jit(solution)/shard_map/nsecd,edh->nsech/dot_general | solution.py:35
  259.7 7.3 %fusion.5 = f32[2,4,8,16,3584]{4,3,2,1,0:T(8,128)} fusion(bf16[4,8,2,16,256]{4,3,1,0,2:T(8,128)(2,1)S(1)} %fusion.29, bf16[2,3584,256]{2,1,0:T(8,128)(2,1)S(1)} %copy-done.2), kind=kOutput, calls=%fused_computation.12 | convolution fusion | flops 1879048192 | bytes 18874368 | tf_op jit(solution)/shard_map/nsech,edh->nsecd/dot_general | solution.py:42
  267.1 11.4 %fusion.1 = bf16[4,8,2,16,3584]{4,3,1,0,2:T(8,128)(2,1)} fusion(f32[2,4,8,16,3584]{4,3,2,1,0:T(8,128)} %fusion.5, bf16[2,3584,256]{2,1,0:T(8,128)(2,1)} %param.12, f32[4,8,2,16,256]{4,3,1,0,2:T(8,128)S(1)} %fusion.17, f32[4,8,2,16,256]{4,3,1,0,2:T(8,128)S(1)} %fusion.14), kind=kOutput, calls=%fused_computation.4 | convolution fusion | flops 1887961088 | bytes 27787264 | tf_op jit(solution)/shard_map/nsech,edh->nsecd/dot_general | solution.py:45
  278.4 0.6 copy-done.5
  279.1 0.6 dynamic-slice
  279.6 154.7 %all-reduce.3.cloned.1.call-done = bf16[4,8,2,16,3584]{4,3,1,0,2:T(8,128)(2,1)} async-done(((bf16[4,8,2,16,3584]{4,3,1,0,2:T(8,128)(2,1)}), bf16[4,8,2,16,3584]{4,3,1,0,2:T(8,128)(2,1)}) %all-reduce.3.cloned.1.call-update) | async-done | bytes 7340048
  434.3 2.3 constant_dynamic-slice_fusion
  436.6 0.1 copy.32
  436.8 47.9 %all_to_all.11 = bf16[1,8,2,16,3584]{4,3,0,2,1:T(8,128)(2,1)S(1)} all-to-all(bf16[1,8,2,16,3584]{4,3,0,2,1:T(8,128)(2,1)S(1)} %copy.32), channel_id=1, replica_groups=mesh['dp'=4,'expert'=8] {'expert'}, dimensions={1} | all-to-all | bytes 3670016 | tf_op jit(solution)/shard_map/all_to_all | solution.py:70
  484.6 1.5 convolution_convert_fusion.1
  (21 shorter events, 0.6 us)
Async XLA Ops:
  6.5 2.5 copy-start
  6.5 235.1 %all-gather.2.cloned.1.call-start = ((), (), s32[]{:S(2)}) async-start(), calls=%async_computation.2 | async-start | bytes 18350080 | tf_op jit(solution)/shard_map/all_gather | solution.py:65
  102.6 331.7 %all-reduce.3.cloned.1.call-start = ((), (), s32[]{:S(2)}) async-start(), calls=%async_computation.3 | async-start | bytes 14680064
  241.6 8.3 %copy-start.4 = (bf16[4,2,8,2,16,3584]{5,4,2,0,3,1:T(8,128)(2,1)S(1)}, bf16[4,2,8,2,16,3584]{5,4,2,0,3,1:T(8,128)(2,1)}, u32[]{:S(2)}) copy-start(bf16[4,2,8,2,16,3584]{5,4,2,0,3,1:T(8,128)(2,1)} %all-gather.2.cloned.1.call-done) | copy-start | bytes 44040196
  249.9 4.3 copy-start.3
  254.2 5.5 %copy-start.2 = (bf16[2,3584,256]{2,1,0:T(8,128)(2,1)S(1)}, bf16[2,3584,256]{2,1,0:T(8,128)(2,1)}, u32[]{:S(2)}) copy-start(bf16[2,3584,256]{2,1,0:T(8,128)(2,1)} %param.11) | copy-start | bytes 11010052
  278.4 0.7 copy-start.5
  436.6 49.5 %copy-start.1 = (bf16[16,3584]{1,0:T(8,128)(2,1)S(1)}, bf16[16,3584]{1,0:T(8,128)(2,1)}, u32[]{:S(2)}) copy-start(bf16[16,3584]{1,0:T(8,128)(2,1)} %param.7) | copy-start | bytes 344068
Sparse Core Ops, SparseCore 0:
  102.7 138.8 all-gather.1
  278.6 155.7 all-reduce.2
where the time goes:
time: 493 us
  waiting for transfers between devices  294 us (60%)
  blocking collectives  137 us (28%)
  matrix products  38.4 us (8%)
  between operations  13.5 us (3%)
  local copies, waits for them, and re-layouts  9.42 us (2%)
    unnamed x3, waiting for transfers between devices  155 us
    all_gather x1, waiting for transfers between devices, on_device(): lax.all_gather(received, 'dp', axis=0, tiled=True)  139 us
    all_to_all x1, blocking collectives, on_device(): lax.all_to_all(tiles, 'expert', split_axis=2, concat_axis=2, tiled=True)  88.9 us
    all_to_all x1, blocking collectives, on_device(): lax.all_to_all(summed.astype(jnp.bfloat16), 'expert', split_axis=1, conca...  47.9 us
    dot_general x1, matrix products, expert_grads(): jnp.einsum('nsech,edh->nsecd', up_grad, w_up, preferred_element_type=jnp....  11.4 us
  transfers between devices with their start and end apart: 2, of which 2 were waited for; matrix products, arithmetic and copies ran while one was open for 0% of the time, Pallas kernels for 0%

commit v1 on v0

--- a/solution.py
+++ b/solution.py
@@ -1,9 +1,268 @@
 import jax
 import jax.numpy as jnp
 from jax import lax
+from jax.experimental import pallas as pl
+from jax.experimental.pallas import tpu as pltpu
 from jax.sharding import PartitionSpec as P
 
 TOPK = 8
+LANES = 128
+MESH = pl.DeviceIdType.MESH
+BF16 = jnp.bfloat16
+F32 = jnp.float32
+COPIES = 64
+NT = (((1,), (1,)), ((), ()))
+
+
+def fused_kernel(
+    tokens_ref, grads_ref, ids_ref, probs_ref, w_gate_ref, w_up_ref, w_down_ref, out_ref,
+    rows_buf, w_cat, w_dn, acc_in, acc_hid, hid_grads, part, core_got, pair_sum,
+    x_got, y_got, send2, got2, column, z_got, send_sems, recv_sems, weight_sems,
+):
+    dp, ex = lax.axis_index("dp"), lax.axis_index("expert")
+    y, x = dp // 2, dp % 2
+    z, c = ex // 2, ex % 2
+    oy, ox, oc = 1 - y, 1 - x, 1 - c
+    to_x, to_y, to_core = (y * 2 + ox, ex), (oy * 2 + x, ex), (dp, z * 2 + oc)
+    to_z = {k: (dp, ((z + k) % 4) * 2 + c) for k in (1, 2, 3)}
+    width = tokens_ref.shape[1]
+    half_w = width // 2
+    local, _, hid = w_gate_ref.shape
+    started = []
+
+    def send(src, dst, device):
+        at = len(started)
+        copy = pltpu.make_async_remote_copy(
+            src_ref=src, dst_ref=dst, send_sem=send_sems.at[at], recv_sem=recv_sems.at[at],
+            device_id=device, device_id_type=MESH,
+        )
+        copy.start()
+        started.append(copy)
+        return copy
+
+    barrier = pltpu.get_barrier_semaphore()
+    for device in (to_x, to_y, to_core, to_z[1], to_z[2], to_z[3]):
+        pl.semaphore_signal(barrier, inc=1, device_id=device, device_id_type=MESH)
+
+    weight_copies = []
+    for e in range(local):
+        for n, ref in enumerate((w_gate_ref, w_up_ref)):
+            weight_copies.append(
+                pltpu.make_async_copy(
+                    ref.at[e], w_cat.at[:, pl.ds((2 * e + n) * hid, hid)], weight_sems.at[2 * e + n]
+                )
+            )
+    weight_copies.append(pltpu.make_async_copy(w_down_ref, w_dn, weight_sems.at[2 * local]))
+    for copy in weight_copies:
+        copy.start()
+
+    lane = lax.broadcasted_iota(jnp.int32, (tokens_ref.shape[0], LANES), 1)
+    weights = jnp.zeros(lane.shape, F32)
+    for k in range(TOPK):
+        weights = weights + jnp.where(ids_ref[:, k : k + 1] == lane, probs_ref[:, k : k + 1], 0.0)
+    high = weights.astype(BF16)
+    rows_buf[y, x, z, c, 0, :, :width] = tokens_ref[...]
+    rows_buf[y, x, z, c, 1, :, :width] = grads_ref[...]
+    rows_buf[y, x, z, c, 0, :, width:] = high
+    rows_buf[y, x, z, c, 1, :, width:] = (weights - high.astype(F32)).astype(BF16)
+
+    pl.semaphore_wait(barrier, 6)
+
+    def block(by, bx, bz):
+        return rows_buf.at[by, bx, bz, c]
+
+    own = block(y, x, z)
+    x_in, y_in, core_col, core_x, core_y, diag_in, core_diag = [], [], [], [], [], [], []
+    x_in.append(send(own, own, to_x))
+    y_in.append(send(own, own, to_y))
+    z_in = {k: send(own, own, to_z[k]) for k in (1, 3, 2)}
+    core_col.append(send(own, own, to_core))
+    order = [z]
+    for k in (1, 3, 2):
+        z_in[k].wait_recv()
+        s = (z + 4 - k) % 4
+        order.append(s)
+        got = block(y, x, s)
+        x_in.append(send(got, got, to_x))
+        y_in.append(send(got, got, to_y))
+        core_col.append(send(got, got, to_core))
+    for i, s in enumerate(order):
+        x_in[i].wait_recv()
+        got = block(y, ox, s)
+        low = got.at[0]
+        diag_in.append(send(low, low, to_y))
+        core_x.append(send(got, got, to_core))
+        y_in[i].wait_recv()
+        got = block(oy, x, s)
+        low = got.at[1]
+        diag_in.append(send(low, low, to_x))
+        core_y.append(send(got, got, to_core))
+    for copy in weight_copies:
+        copy.wait()
+    for copy in core_col + core_x:
+        copy.wait_recv()
+
+    rows = 16 * tokens_ref.shape[0]
+    k_tile = 512
+    o_tile = 256
+
+    def hidden(by):
+        acc_in[...] = jnp.zeros_like(acc_in)
+        acc_hid[...] = jnp.zeros_like(acc_hid)
+
+        @pl.loop(0, width // k_tile)
+        def _(k):
+            cols = pl.ds(pl.multiple_of(k * k_tile, k_tile), k_tile)
+            x_rows = rows_buf[by, :, :, :, 0, :, cols].reshape(rows, k_tile)
+            g_rows = rows_buf[by, :, :, :, 1, :, cols].reshape(rows, k_tile)
+            acc_in[...] += jnp.dot(x_rows, w_cat[cols, :], preferred_element_type=F32)
+            down = w_dn[:, :, cols].reshape(local * hid, k_tile)
+            acc_hid[...] += lax.dot_general(g_rows, down, NT, preferred_element_type=F32)
+
+        tail = pl.ds(width, LANES)
+        wts = rows_buf[by, :, :, :, 0, :, tail].reshape(rows, LANES).astype(F32)
+        wts = wts + rows_buf[by, :, :, :, 1, :, tail].reshape(rows, LANES).astype(F32)
+        which = lax.broadcasted_iota(jnp.int32, (rows, LANES), 1)
+        for e in range(local):
+            scale = jnp.sum(jnp.where(which == ex * local + e, wts, 0.0), axis=1, keepdims=True)
+            gate = acc_in[:, 2 * e * hid : (2 * e + 1) * hid]
+            up = acc_in[:, (2 * e + 1) * hid : (2 * e + 2) * hid]
+            grad = acc_hid[:, e * hid : (e + 1) * hid] * scale
+            s = jax.nn.sigmoid(gate)
+            hid_grads[:, 2 * e * hid : (2 * e + 1) * hid] = (
+                grad * up * s * (1.0 + gate * (1.0 - s))
+            ).astype(BF16)
+            hid_grads[:, (2 * e + 1) * hid : (2 * e + 2) * hid] = (grad * gate * s).astype(BF16)
+
+    def project(h, half):
+        @pl.loop(0, half_w // o_tile)
+        def _(j):
+            local_cols = pl.ds(pl.multiple_of(j * o_tile, o_tile), o_tile)
+            w_rows = pl.ds(pl.multiple_of(half * half_w + j * o_tile, o_tile), o_tile)
+            value = lax.dot_general(hid_grads[...], w_cat[w_rows, :], NT, preferred_element_type=F32)
+            value = value.astype(BF16).reshape(2, 4, 2, rows // 16, o_tile)
+            part[h, half, 0, :, :, :, local_cols] = value[:, :, 0]
+            part[h, half, 1, :, :, :, local_cols] = value[:, :, 1]
+
+        return send(part.at[h, half, oc], core_got.at[h, half], to_core)
+
+    def add_cores(h, half, copy):
+        copy.wait_recv()
+
+        @pl.loop(0, 4)
+        def _(b):
+            pair_sum[h, half, :, b] = (
+                part[h, half, c, :, b].astype(F32) + core_got[h, half, :, b].astype(F32)
+            ).astype(BF16)
+
+    hidden(y)
+    core0 = [project(0, 0), project(0, 1)]
+    for i, s in enumerate(order):
+        for n in range(2):
+            diag_in[2 * i + n].wait_recv()
+            got = block(oy, ox, s).at[n]
+            core_diag.append(send(got, got, to_core))
+    add_cores(0, 0, core0[0])
+    rx0 = send(pair_sum.at[0, 0, ox], x_got.at[0], to_x)
+    add_cores(0, 1, core0[1])
+    for copy in core_y + core_diag:
+        copy.wait_recv()
+    hidden(oy)
+    core1b = project(1, 1)
+    core1a = project(1, 0)
+    add_cores(1, 1, core1b)
+    ry = send(pair_sum.at[1, 1], y_got, to_y)
+    add_cores(1, 0, core1a)
+    rx1 = send(pair_sum.at[1, 0, ox], x_got.at[1], to_x)
+
+    rx1.wait_recv()
+
+    @pl.loop(0, 4)
+    def _(b):
+        send2[0, b] = (pair_sum[1, 0, x, b].astype(F32) + x_got[1, b].astype(F32)).astype(BF16)
+
+    ry2 = send(send2.at[0], got2.at[0], to_y)
+    ry.wait_recv()
+
+    @pl.loop(0, 4)
+    def _(b):
+        send2[1, b] = (pair_sum[0, 1, ox, b].astype(F32) + y_got[ox, b].astype(F32)).astype(BF16)
+
+    rx2 = send(send2.at[1], got2.at[1], to_x)
+    rx0.wait_recv()
+    ry2.wait_recv()
+
+    @pl.loop(0, 4)
+    def _(b):
+        column[0, b] = (
+            pair_sum[0, 0, x, b].astype(F32) + x_got[0, b].astype(F32) + got2[0, b].astype(F32)
+        ).astype(BF16)
+
+    z_out = [[], []]
+    for k in (2, 1, 3):
+        z_out[0].append(send(column.at[0, (z + k) % 4], z_got.at[0, k - 1], to_z[k]))
+    rx2.wait_recv()
+
+    @pl.loop(0, 4)
+    def _(b):
+        column[1, b] = (
+            pair_sum[0, 1, x, b].astype(F32) + y_got[x, b].astype(F32) + got2[1, b].astype(F32)
+        ).astype(BF16)
+
+    for k in (2, 1, 3):
+        z_out[1].append(send(column.at[1, (z + k) % 4], z_got.at[1, k - 1], to_z[k]))
+    for half in range(2):
+        for copy in z_out[half]:
+            copy.wait_recv()
+        total = column[half, z].astype(F32)
+        for k in range(3):
+            total = total + z_got[half, k].astype(F32)
+        out_ref[:, half * half_w : (half + 1) * half_w] = total.astype(BF16)
+    for copy in started:
+        copy.wait_send()
+
+
+def fused(tokens, out_grad, route_ids, route_probs, w_gate, w_up, w_down):
+    toks, width = tokens.shape
+    local, _, hid = w_gate.shape
+    half_w = width // 2
+    rows = 16 * toks
+    vmem = pl.BlockSpec(memory_space=pltpu.VMEM)
+    hbm = pl.BlockSpec(memory_space=pl.ANY)
+    scratch = [
+        pltpu.VMEM((2, 2, 4, 2, 2, toks, width + LANES), BF16),
+        pltpu.VMEM((width, 2 * local * hid), BF16),
+        pltpu.VMEM((local, hid, width), BF16),
+        pltpu.VMEM((rows, 2 * local * hid), F32),
+        pltpu.VMEM((rows, local * hid), F32),
+        pltpu.VMEM((rows, 2 * local * hid), BF16),
+        pltpu.VMEM((2, 2, 2, 2, 4, toks, half_w), BF16),
+        pltpu.VMEM((2, 2, 2, 4, toks, half_w), BF16),
+        pltpu.VMEM((2, 2, 2, 4, toks, half_w), BF16),
+        pltpu.VMEM((2, 4, toks, half_w), BF16),
+        pltpu.VMEM((2, 4, toks, half_w), BF16),
+        pltpu.VMEM((2, 4, toks, half_w), BF16),
+        pltpu.VMEM((2, 4, toks, half_w), BF16),
+        pltpu.VMEM((2, 4, toks, half_w), BF16),
+        pltpu.VMEM((2, 3, toks, half_w), BF16),
+        pltpu.SemaphoreType.DMA((COPIES,)),
+        pltpu.SemaphoreType.DMA((COPIES,)),
+        pltpu.SemaphoreType.DMA((2 * local + 1,)),
+    ]
+    flops = 2 * 2 * rows * width * local * hid * 5
+    return pl.pallas_call(
+        fused_kernel,
+        out_shape=jax.ShapeDtypeStruct((toks, width), BF16),
+        in_specs=[vmem, vmem, vmem, vmem, hbm, hbm, hbm],
+        out_specs=vmem,
+        scratch_shapes=scratch,
+        compiler_params=pltpu.CompilerParams(
+            collective_id=0, has_side_effects=True, vmem_limit_bytes=56 * 1024 * 1024
+        ),
+        cost_estimate=pl.CostEstimate(
+            flops=flops, bytes_accessed=6 * local * hid * width, transcendentals=2 * rows * local * hid
+        ),
+    )(tokens, out_grad, route_ids, route_probs, w_gate, w_up, w_down)
 
 
 def slot_matches(flat_ids, experts, capacity):
@@ -85,6 +344,15 @@
         P("expert", None, "dp"),
         P("expert", "dp", None),
     )
+    whole_block = dict(mesh.shape) == {"dp": 4, "expert": 8}
+
+    def chosen(tokens, out_grad, route_ids, route_probs, w_gate, w_up, w_down):
+        experts = w_gate.shape[0] * mesh.shape["expert"]
+        dense = 2 * tokens.shape[0] * TOPK // experts >= tokens.shape[0]
+        fits = tokens.shape[0] == 16 and experts <= LANES
+        step = fused if whole_block and dense and fits else on_device
+        return step(tokens, out_grad, route_ids, route_probs, w_gate, w_up, w_down)
+
     return jax.shard_map(
-        on_device, mesh=mesh, in_specs=placed, out_specs=P(("dp", "expert"), None), check_vma=False
-    )
+        chosen, mesh=mesh, in_specs=placed, out_specs=P(("dp", "expert"), None), check_vma=False
+    )

time: 493 us -> 93.2 us (0.19)
  waiting for transfers between devices: 294 us -> 0 us
  blocking collectives: 137 us -> 0 us
  Pallas kernels: 0 us -> 88.7 us
  matrix products: 38.4 us -> 0 us
  between operations: 13.5 us -> 0.01 us
  local copies, waits for them, and re-layouts: 9.42 us -> 4.26 us
    unnamed x3 -> x0, waiting for transfers between devices: 155 us -> none
    all_gather x1 -> x0, waiting for transfers between devices: 139 us -> none  [on_device(): lax.all_gather(received, 'dp', axis=0, tiled=True)]
    all_to_all x2 -> x0, blocking collectives: 137 us -> none  [the longest x1 88.9 us: on_device(): lax.all_to_all(tiles, 'expert', split_axis=2, concat_axis=2, tiled=True)]
    pallas_call x0 -> x1, Pallas kernels: none -> 88.7 us  [fused(): pl.pallas_call(fused_kernel, out_shape=jax.ShapeDtypeStruct((toks, width)...]
    dot_general x8 -> x0, matrix products: 38.4 us -> none  [the longest x1 11.4 us: expert_grads(): jnp.einsum('nsech,edh->nsecd', up_grad, w_up, preferred_element_type=jnp....]
  transfers between devices with their start and end apart: 2 -> 0, of which waited for: 2 -> 0; matrix products, arithmetic and copies ran while one was open for 0% -> 0% of each run, Pallas kernels for 0% -> 0%
where the time goes in v1:
time: 93.2 us; the launch traced here: 92.9 us
  Pallas kernels  88.7 us (95%)
  local copies, waits for them, and re-layouts  4.26 us (5%)
    pallas_call x1, Pallas kernels, fused(): pl.pallas_call(fused_kernel, out_shape=jax.ShapeDtypeStruct((toks, width)...  88.7 us
    unnamed x3, local copies, waits for them, and re-layouts  4.26 us

profile of v1, /device:TPU:0, one launch (start us, length us, event | category | flops | bytes accessed | tf_op | source)
XLA Modules:
  0.0 92.9 jit_solution(12207420018522755902)
XLA Ops:
  0.0 1.4 %copy.8.ids_ref = s32[16,8]{1,0:T(8,128)} copy(s32[16,8]{0,1:T(8,128)} %param.9) | data formatting | bytes 1024 | tf_op args[2]
  1.4 1.4 %copy.9.probs_ref = f32[16,8]{1,0:T(8,128)} copy(f32[16,8]{0,1:T(8,128)} %param.10) | data formatting | bytes 1024 | tf_op args[3]
  2.7 88.7 %shard_map.73 = bf16[16,3584]{1,0:T(8,128)(2,1)} custom-call(bf16[16,3584]{1,0:T(8,128)(2,1)} %tokens_ref.1, bf16[16,3584]{1,0:T(8,128)(2,1)} %grads_ref.1, s32[16,8]{1,0:T(8,128)} %copy.8.ids_ref, f32[16,8]{1,0:T(8,128)} %copy.9.probs_ref, bf16[2,3584,256]{2,1,0:T(8,128)(2,1)} %w_gate_ref.1, bf16[2,3584,256]{2,1,0:T(8,128)(2,1)} %w_up_ref.1, ...), custom_call_target="tpu_custom_call" | custom-call | flops 9395240960 | bytes 11010048 | tf_op jit(solution)/shard_map/pallas_call | solution.py:253
  91.4 1.6 %copy.11 = bf16[16,3584]{1,0:T(8,128)(2,1)} copy(bf16[16,3584]{1,0:T(8,128)(2,1)} %shard_map.73) | data formatting | bytes 229376

commit v2 on v0

--- a/solution.py
+++ b/solution.py
@@ -1,9 +1,278 @@
 import jax
 import jax.numpy as jnp
 from jax import lax
+from jax.experimental import pallas as pl
+from jax.experimental.pallas import tpu as pltpu
 from jax.sharding import PartitionSpec as P
 
 TOPK = 8
+LANES = 128
+MESH = pl.DeviceIdType.MESH
+BF16 = jnp.bfloat16
+F32 = jnp.float32
+COPIES = 80
+NT = (((1,), (1,)), ((), ()))
+
+
+def fused_kernel(
+    tokens_ref, grads_ref, ids_ref, probs_ref, w_gate_ref, w_up_ref, w_down_ref, out_ref,
+    rows_buf, w_cat, w_dn, acc_in, acc_hid, hid_grads, part, core_got, sum_a, sum_b,
+    x_got, y_got, send2, got2, column, z_got, send_sems, recv_sems, local_sems,
+):
+    dp, ex = lax.axis_index("dp"), lax.axis_index("expert")
+    y, x = dp // 2, dp % 2
+    z, c = ex // 2, ex % 2
+    oy, ox, oc = 1 - y, 1 - x, 1 - c
+    to_x, to_y, to_core = (y * 2 + ox, ex), (oy * 2 + x, ex), (dp, z * 2 + oc)
+    to_z = {k: (dp, ((z + k) % 4) * 2 + c) for k in (1, 2, 3)}
+    toks, width = tokens_ref.shape
+    half_w = width // 2
+    local, _, hid = w_gate_ref.shape
+    started = []
+
+    def send(src, dst, device):
+        at = len(started)
+        copy = pltpu.make_async_remote_copy(
+            src_ref=src, dst_ref=dst, send_sem=send_sems.at[at], recv_sem=recv_sems.at[at],
+            device_id=device, device_id_type=MESH,
+        )
+        copy.start()
+        started.append(copy)
+        return copy
+
+    barrier = pltpu.get_barrier_semaphore()
+    for device in (to_x, to_y, to_core, to_z[1], to_z[2], to_z[3]):
+        pl.semaphore_signal(barrier, inc=1, device_id=device, device_id_type=MESH)
+
+    own = rows_buf.at[z, y, x, c]
+    row_copies = [
+        pltpu.make_async_copy(ref, own.at[n, :, pl.ds(0, width)], local_sems.at[n])
+        for n, ref in enumerate((tokens_ref, grads_ref))
+    ]
+    weight_copies = []
+    for e in range(local):
+        for n, ref in enumerate((w_gate_ref, w_up_ref)):
+            weight_copies.append(
+                pltpu.make_async_copy(
+                    ref.at[e],
+                    w_cat.at[:, pl.ds((2 * e + n) * hid, hid)],
+                    local_sems.at[2 + 2 * e + n],
+                )
+            )
+    weight_copies.append(pltpu.make_async_copy(w_down_ref, w_dn, local_sems.at[2 + 2 * local]))
+    for copy in row_copies + weight_copies:
+        copy.start()
+
+    expert = lax.broadcasted_iota(jnp.int32, (LANES, toks), 0)
+    weights = jnp.zeros(expert.shape, F32)
+    for k in range(TOPK):
+        weights = weights + jnp.where(ids_ref[k : k + 1, :] == expert, probs_ref[k : k + 1, :], 0.0)
+    high = weights.astype(BF16)
+    low = (weights - high.astype(F32)).astype(BF16)
+    diagonal = lax.broadcasted_iota(jnp.int32, (toks, toks), 0) == lax.broadcasted_iota(
+        jnp.int32, (toks, toks), 1
+    )
+    eye = jnp.where(diagonal, 1.0, 0.0).astype(BF16)
+    for copy in row_copies:
+        copy.wait()
+    for n, value in enumerate((high, low)):
+        turned = lax.dot_general(eye, value, NT, preferred_element_type=F32)
+        rows_buf[z, y, x, c, n, :, width:] = turned.astype(BF16)
+
+    pl.semaphore_wait(barrier, 6)
+
+    shifts = (0, 1, 3, 2)
+    order = [(z + 4 - k) % 4 for k in shifts]
+    x_in, y_in, z_in, diag_in = {}, {}, {}, {}
+    core_in = {i: [] for i in range(4)}
+    core_sum, stage1, stage2, z_out = {}, {}, {}, {}
+
+    def to_plane(i):
+        got = rows_buf.at[order[i], y, x, c]
+        x_in[i] = send(got, got, to_x)
+        y_in[i] = send(got, got, to_y)
+        if i == 0:
+            for k in shifts[1:]:
+                z_in[k] = send(own, own, to_z[k])
+        core_in[i].append(send(got, got, to_core))
+
+    def from_z(i):
+        z_in[shifts[i]].wait_recv()
+        to_plane(i)
+
+    def relay(i):
+        x_in[i].wait_recv()
+        got = rows_buf.at[order[i], y, ox, c]
+        first = send(got.at[0], got.at[0], to_y)
+        core_in[i].append(send(got, got, to_core))
+        y_in[i].wait_recv()
+        got = rows_buf.at[order[i], oy, x, c]
+        diag_in[i] = (first, send(got.at[1], got.at[1], to_x))
+        core_in[i].append(send(got, got, to_core))
+
+    def share_diagonal(i):
+        for n in range(2):
+            diag_in[i][n].wait_recv()
+            got = rows_buf.at[order[i], oy, ox, c, n]
+            core_in[i].append(send(got, got, to_core))
+
+    rows = 8 * toks
+    k_tile = width // 2
+
+    def compute(i):
+        for copy in core_in[i]:
+            copy.wait_recv()
+        s = order[i]
+        acc_in[...] = jnp.zeros_like(acc_in)
+        acc_hid[...] = jnp.zeros_like(acc_hid)
+
+        @pl.loop(0, width // k_tile)
+        def _(k):
+            cols = pl.ds(pl.multiple_of(k * k_tile, LANES), k_tile)
+            x_rows = rows_buf[s, :, :, :, 0, :, cols].reshape(rows, k_tile)
+            g_rows = rows_buf[s, :, :, :, 1, :, cols].reshape(rows, k_tile)
+            acc_in[...] += jnp.dot(x_rows, w_cat[cols, :], preferred_element_type=F32)
+            down = w_dn[:, :, cols].reshape(local * hid, k_tile)
+            acc_hid[...] += lax.dot_general(g_rows, down, NT, preferred_element_type=F32)
+
+        tail = pl.ds(width, LANES)
+        wts = rows_buf[s, :, :, :, 0, :, tail].reshape(rows, LANES).astype(F32)
+        wts = wts + rows_buf[s, :, :, :, 1, :, tail].reshape(rows, LANES).astype(F32)
+        which = lax.broadcasted_iota(jnp.int32, (rows, LANES), 1)
+        for e in range(local):
+            scale = jnp.sum(jnp.where(which == ex * local + e, wts, 0.0), axis=1, keepdims=True)
+            gate = acc_in[:, 2 * e * hid : (2 * e + 1) * hid]
+            up = acc_in[:, (2 * e + 1) * hid : (2 * e + 2) * hid]
+            grad = acc_hid[:, e * hid : (e + 1) * hid] * scale
+            sig = jax.nn.sigmoid(gate)
+            hid_grads[:, 2 * e * hid : (2 * e + 1) * hid] = (
+                grad * up * sig * (1.0 + gate * (1.0 - sig))
+            ).astype(BF16)
+            hid_grads[:, (2 * e + 1) * hid : (2 * e + 2) * hid] = (grad * gate * sig).astype(BF16)
+        for half in range(2):
+            w_rows = pl.ds(half * half_w, half_w)
+            value = lax.dot_general(hid_grads[...], w_cat[w_rows, :], NT, preferred_element_type=F32)
+            value = value.astype(BF16).reshape(2, 2, 2, toks, half_w)
+            part[i, half, 0] = value[:, :, 0]
+            part[i, half, 1] = value[:, :, 1]
+            core_sum[i, half] = send(part.at[i, half, oc], core_got.at[i, half], to_core)
+
+    def add(*refs):
+        total = refs[0][...].astype(F32)
+        for ref in refs[1:]:
+            total = total + ref[...].astype(F32)
+        return total.astype(BF16)
+
+    def reduce1(i):
+        core_sum[i, 0].wait_recv()
+        for by in range(2):
+            for bx in range(2):
+                sum_a[i, bx, by] = add(part.at[i, 0, c, by, bx], core_got.at[i, 0, by, bx])
+        first = send(sum_a.at[i, ox], x_got.at[i], to_x)
+        core_sum[i, 1].wait_recv()
+        for by in range(2):
+            for bx in range(2):
+                sum_b[i, by, bx] = add(part.at[i, 1, c, by, bx], core_got.at[i, 1, by, bx])
+        stage1[i] = (first, send(sum_b.at[i, oy], y_got.at[i], to_y))
+
+    def reduce2(i):
+        stage1[i][0].wait_recv()
+        send2[i, 0] = add(sum_a.at[i, x, oy], x_got.at[i, oy])
+        first = send(send2.at[i, 0], got2.at[i, 0], to_y)
+        stage1[i][1].wait_recv()
+        send2[i, 1] = add(sum_b.at[i, y, ox], y_got.at[i, ox])
+        stage2[i] = (first, send(send2.at[i, 1], got2.at[i, 1], to_x))
+
+    def reduce3(i):
+        stage2[i][0].wait_recv()
+        column[i, 0] = add(sum_a.at[i, x, y], x_got.at[i, y], got2.at[i, 0])
+        stage2[i][1].wait_recv()
+        column[i, 1] = add(sum_b.at[i, y, x], y_got.at[i, x], got2.at[i, 1])
+        if i > 0:
+            z_out[i] = send(column.at[i], z_got.at[i - 1], to_z[4 - shifts[i]])
+
+    to_plane(0)
+    from_z(1)
+    relay(0)
+    from_z(2)
+    relay(1)
+    share_diagonal(0)
+    for copy in weight_copies:
+        copy.wait()
+    compute(0)
+    from_z(3)
+    relay(2)
+    share_diagonal(1)
+    reduce1(0)
+    compute(1)
+    relay(3)
+    share_diagonal(2)
+    reduce1(1)
+    reduce2(0)
+    compute(2)
+    share_diagonal(3)
+    reduce1(2)
+    reduce2(1)
+    reduce3(0)
+    compute(3)
+    reduce1(3)
+    reduce2(2)
+    reduce3(1)
+    reduce2(3)
+    reduce3(2)
+    reduce3(3)
+    for i in (1, 2, 3):
+        z_out[i].wait_recv()
+    for half in range(2):
+        out_ref[:, half * half_w : (half + 1) * half_w] = add(
+            column.at[0, half], z_got.at[0, half], z_got.at[1, half], z_got.at[2, half]
+        )
+    for copy in started:
+        copy.wait_send()
+
+
+def fused(tokens, out_grad, route_ids, route_probs, w_gate, w_up, w_down):
+    toks, width = tokens.shape
+    local, _, hid = w_gate.shape
+    half_w = width // 2
+    rows = 8 * toks
+    vmem = pl.BlockSpec(memory_space=pltpu.VMEM)
+    hbm = pl.BlockSpec(memory_space=pl.ANY)
+    scratch = [
+        pltpu.VMEM((4, 2, 2, 2, 2, toks, width + LANES), BF16),
+        pltpu.VMEM((width, 2 * local * hid), BF16),
+        pltpu.VMEM((local, hid, width), BF16),
+        pltpu.VMEM((rows, 2 * local * hid), F32),
+        pltpu.VMEM((rows, local * hid), F32),
+        pltpu.VMEM((rows, 2 * local * hid), BF16),
+        pltpu.VMEM((4, 2, 2, 2, 2, toks, half_w), BF16),
+        pltpu.VMEM((4, 2, 2, 2, toks, half_w), BF16),
+        pltpu.VMEM((4, 2, 2, toks, half_w), BF16),
+        pltpu.VMEM((4, 2, 2, toks, half_w), BF16),
+        pltpu.VMEM((4, 2, toks, half_w), BF16),
+        pltpu.VMEM((4, 2, toks, half_w), BF16),
+        pltpu.VMEM((4, 2, toks, half_w), BF16),
+        pltpu.VMEM((4, 2, toks, half_w), BF16),
+        pltpu.VMEM((4, 2, toks, half_w), BF16),
+        pltpu.VMEM((3, 2, toks, half_w), BF16),
+        pltpu.SemaphoreType.DMA((COPIES,)),
+        pltpu.SemaphoreType.DMA((COPIES,)),
+        pltpu.SemaphoreType.DMA((2 * local + 3,)),
+    ]
+    flops = 2 * 4 * rows * width * local * hid * 5
+    return pl.pallas_call(
+        fused_kernel,
+        out_shape=jax.ShapeDtypeStruct((toks, width), BF16),
+        in_specs=[hbm, hbm, vmem, vmem, hbm, hbm, hbm],
+        out_specs=vmem,
+        scratch_shapes=scratch,
+        compiler_params=pltpu.CompilerParams(
+            collective_id=0, has_side_effects=True, vmem_limit_bytes=56 * 1024 * 1024
+        ),
+        cost_estimate=pl.CostEstimate(
+            flops=flops, bytes_accessed=6 * local * hid * width, transcendentals=4 * rows * local * hid
+        ),
+    )(tokens, out_grad, route_ids.T, route_probs.T, w_gate, w_up, w_down)
 
 
 def slot_matches(flat_ids, experts, capacity):
@@ -85,6 +354,15 @@
         P("expert", None, "dp"),
         P("expert", "dp", None),
     )
+    whole_block = dict(mesh.shape) == {"dp": 4, "expert": 8}
+
+    def chosen(tokens, out_grad, route_ids, route_probs, w_gate, w_up, w_down):
+        experts = w_gate.shape[0] * mesh.shape["expert"]
+        dense = 2 * tokens.shape[0] * TOPK // experts >= tokens.shape[0]
+        fits = tokens.shape[0] == 16 and experts <= LANES
+        step = fused if whole_block and dense and fits else on_device
+        return step(tokens, out_grad, route_ids, route_probs, w_gate, w_up, w_down)
+
     return jax.shard_map(
-        on_device, mesh=mesh, in_specs=placed, out_specs=P(("dp", "expert"), None), check_vma=False
-    )
+        chosen, mesh=mesh, in_specs=placed, out_specs=P(("dp", "expert"), None), check_vma=False
+    )

time: 493 us -> 79.5 us (0.16)
  waiting for transfers between devices: 294 us -> 0 us
  blocking collectives: 137 us -> 0 us
  Pallas kernels: 0 us -> 77.7 us
  matrix products: 38.4 us -> 0 us
  between operations: 13.5 us -> 0.01 us
  local copies, waits for them, and re-layouts: 9.42 us -> 1.55 us
    unnamed x3 -> x0, waiting for transfers between devices: 155 us -> none
    all_gather x1 -> x0, waiting for transfers between devices: 139 us -> none  [on_device(): lax.all_gather(received, 'dp', axis=0, tiled=True)]
    all_to_all x2 -> x0, blocking collectives: 137 us -> none  [the longest x1 88.9 us: on_device(): lax.all_to_all(tiles, 'expert', split_axis=2, concat_axis=2, tiled=True)]
    pallas_call x0 -> x1, Pallas kernels: none -> 77.7 us  [fused(): pl.pallas_call(fused_kernel, out_shape=jax.ShapeDtypeStruct((toks, width)...]
    dot_general x8 -> x0, matrix products: 38.4 us -> none  [the longest x1 11.4 us: expert_grads(): jnp.einsum('nsech,edh->nsecd', up_grad, w_up, preferred_element_type=jnp....]
    unnamed x16 -> x1, local copies, waits for them, and re-layouts: 7.02 us -> 1.55 us
  transfers between devices with their start and end apart: 2 -> 0, of which waited for: 2 -> 0; matrix products, arithmetic and copies ran while one was open for 0% -> 0% of each run, Pallas kernels for 0% -> 0%
where the time goes in v2:
time: 79.5 us; the launch traced here: 79.3 us
  Pallas kernels  77.7 us (98%)
  local copies, waits for them, and re-layouts  1.55 us (2%)
    pallas_call x1, Pallas kernels, fused(): pl.pallas_call(fused_kernel, out_shape=jax.ShapeDtypeStruct((toks, width)...  77.7 us

profile of v2, /device:TPU:0, one launch (start us, length us, event | category | flops | bytes accessed | tf_op | source)
XLA Modules:
  0.0 79.3 jit_solution(8891519724490028458)
XLA Ops:
  0.0 77.7 %shard_map.73 = bf16[16,3584]{1,0:T(8,128)(2,1)} custom-call(bf16[16,3584]{1,0:T(8,128)(2,1)} %tokens_ref.1, bf16[16,3584]{1,0:T(8,128)(2,1)} %grads_ref.1, s32[8,16]{1,0:T(8,128)} %bitcast.2, f32[8,16]{1,0:T(8,128)} %bitcast.3, bf16[2,3584,256]{2,1,0:T(8,128)(2,1)} %w_gate_ref.1, bf16[2,3584,256]{2,1,0:T(8,128)(2,1)} %w_up_ref.1, ...), custom_call_target="tpu_custom_call" | custom-call | flops 9395240960 | bytes 11010048 | tf_op jit(solution)/shard_map/pallas_call | solution.py:263
  77.7 1.6 %copy.9 = bf16[16,3584]{1,0:T(8,128)(2,1)} copy(bf16[16,3584]{1,0:T(8,128)(2,1)} %shard_map.73) | data formatting | bytes 229376

commit v3 on v2

--- a/solution.py
+++ b/solution.py
@@ -17,7 +17,7 @@
 def fused_kernel(
     tokens_ref, grads_ref, ids_ref, probs_ref, w_gate_ref, w_up_ref, w_down_ref, out_ref,
     rows_buf, w_cat, w_dn, acc_in, acc_hid, hid_grads, part, core_got, sum_a, sum_b,
-    x_got, y_got, send2, got2, column, z_got, send_sems, recv_sems, local_sems,
+    x_got, y_got, send2, got2, column, z_got, send_sems, recv_sems, z_send_sems, z_recv_sems, local_sems,
 ):
     dp, ex = lax.axis_index("dp"), lax.axis_index("expert")
     y, x = dp // 2, dp % 2
@@ -81,23 +81,47 @@
 
     pl.semaphore_wait(barrier, 6)
 
-    shifts = (0, 1, 3, 2)
-    order = [(z + 4 - k) % 4 for k in shifts]
-    x_in, y_in, z_in, diag_in = {}, {}, {}, {}
+    upper = z // 2
+    inner = z + upper * (3 - 2 * z)
+    order = [z] + [f + upper * (3 - 2 * f) for f in (1 - inner, 2, 3)]
+    x_in, y_in, diag_in = {}, {}, {}
+    z_sent = []
     core_in = {i: [] for i in range(4)}
-    core_sum, stage1, stage2, z_out = {}, {}, {}, {}
+    core_sum, stage1, stage2 = {}, {}, {}
+
+    def z_copy(src, dst, target, source, kind, at):
+        return pltpu.make_async_remote_copy(
+            src_ref=src, dst_ref=dst, send_sem=z_send_sems.at[kind, at],
+            recv_sem=z_recv_sems.at[kind, source],
+            device_id=(dp, target * 2 + c), device_id_type=MESH,
+        )
+
+    def along_z(source, target, at):
+        got = rows_buf.at[source, y, x, c]
+        copy = z_copy(got, got, target, source, 0, at)
+        there = jnp.logical_and(target >= 0, target <= 3)
+
+        @pl.when(there)
+        def _():
+            copy.start()
+
+        z_sent.append((copy, there))
 
     def to_plane(i):
         got = rows_buf.at[order[i], y, x, c]
         x_in[i] = send(got, got, to_x)
         y_in[i] = send(got, got, to_y)
         if i == 0:
-            for k in shifts[1:]:
-                z_in[k] = send(own, own, to_z[k])
+            along_z(z, z - 1, 0)
+            along_z(z, z + 1, 4)
         core_in[i].append(send(got, got, to_core))
 
     def from_z(i):
-        z_in[shifts[i]].wait_recv()
+        s = order[i]
+        got = rows_buf.at[s, y, x, c]
+        z_copy(got, got, s, s, 0, 0).wait_recv()
+        up = (z + 4 - s) // 4
+        along_z(s, z + 2 * up - 1, i)
         to_plane(i)
 
     def relay(i):
@@ -189,7 +213,9 @@
         stage2[i][1].wait_recv()
         column[i, 1] = add(sum_b.at[i, y, x], y_got.at[i, x], got2.at[i, 1])
         if i > 0:
-            z_out[i] = send(column.at[i], z_got.at[i - 1], to_z[4 - shifts[i]])
+            copy = z_copy(column.at[i], z_got.at[z], order[i], z, 1, i)
+            copy.start()
+            z_sent.append((copy, None))
 
     to_plane(0)
     from_z(1)
@@ -221,14 +247,23 @@
     reduce2(3)
     reduce3(2)
     reduce3(3)
-    for i in (1, 2, 3):
-        z_out[i].wait_recv()
+    for s in order[1:]:
+        got = z_got.at[s]
+        z_copy(got, got, s, s, 1, 0).wait_recv()
     for half in range(2):
         out_ref[:, half * half_w : (half + 1) * half_w] = add(
-            column.at[0, half], z_got.at[0, half], z_got.at[1, half], z_got.at[2, half]
+            column.at[0, half], *[z_got.at[s, half] for s in order[1:]]
         )
     for copy in started:
         copy.wait_send()
+    for copy, there in z_sent:
+        if there is None:
+            copy.wait_send()
+        else:
+
+            @pl.when(there)
+            def _(copy=copy):
+                copy.wait_send()
 
 
 def fused(tokens, out_grad, route_ids, route_probs, w_gate, w_up, w_down):
@@ -254,9 +289,11 @@
         pltpu.VMEM((4, 2, toks, half_w), BF16),
         pltpu.VMEM((4, 2, toks, half_w), BF16),
         pltpu.VMEM((4, 2, toks, half_w), BF16),
-        pltpu.VMEM((3, 2, toks, half_w), BF16),
+        pltpu.VMEM((4, 2, toks, half_w), BF16),
         pltpu.SemaphoreType.DMA((COPIES,)),
         pltpu.SemaphoreType.DMA((COPIES,)),
+        pltpu.SemaphoreType.DMA((2, 5)),
+        pltpu.SemaphoreType.DMA((2, 4)),
         pltpu.SemaphoreType.DMA((2 * local + 3,)),
     ]
     flops = 2 * 4 * rows * width * local * hid * 5

time: 79.5 us -> 78.7 us (0.990)
  no operation moved by 1% of the time
where the time goes in v3:
time: 78.7 us; the launch traced here: 78.5 us
  Pallas kernels  77 us (98%)
  local copies, waits for them, and re-layouts  1.55 us (2%)
    pallas_call x1, Pallas kernels, fused(): pl.pallas_call(fused_kernel, out_shape=jax.ShapeDtypeStruct((toks, width)...  77 us

profile of v3, /device:TPU:0, one launch (start us, length us, event | category | flops | bytes accessed | tf_op | source)
XLA Modules:
  0.0 78.5 jit_solution(6121797935183937677)
XLA Ops:
  0.0 77.0 %shard_map.73 = bf16[16,3584]{1,0:T(8,128)(2,1)} custom-call(bf16[16,3584]{1,0:T(8,128)(2,1)} %tokens_ref.1, bf16[16,3584]{1,0:T(8,128)(2,1)} %grads_ref.1, s32[8,16]{1,0:T(8,128)} %bitcast.2, f32[8,16]{1,0:T(8,128)} %bitcast.3, bf16[2,3584,256]{2,1,0:T(8,128)(2,1)} %w_gate_ref.1, bf16[2,3584,256]{2,1,0:T(8,128)(2,1)} %w_up_ref.1, ...), custom_call_target="tpu_custom_call" | custom-call | flops 9395240960 | bytes 11010048 | tf_op jit(solution)/shard_map/pallas_call | solution.py:300
  77.0 1.6 %copy.9 = bf16[16,3584]{1,0:T(8,128)(2,1)} copy(bf16[16,3584]{1,0:T(8,128)(2,1)} %shard_map.73) | data formatting | bytes 229376

commit v4 on v3

--- a/solution.py
+++ b/solution.py
@@ -16,7 +16,7 @@
 
 def fused_kernel(
     tokens_ref, grads_ref, ids_ref, probs_ref, w_gate_ref, w_up_ref, w_down_ref, out_ref,
-    rows_buf, w_cat, w_dn, acc_in, acc_hid, hid_grads, part, core_got, sum_a, sum_b,
+    rows_buf, w_cat, w_dn, w_cat_t, w_dn_t, acc_in, acc_hid, hid_grads, part, core_got, sum_a, sum_b,
     x_got, y_got, send2, got2, column, z_got, send_sems, recv_sems, z_send_sems, z_recv_sems, local_sems,
 ):
     dp, ex = lax.axis_index("dp"), lax.axis_index("expert")
@@ -59,7 +59,7 @@
                     local_sems.at[2 + 2 * e + n],
                 )
             )
-    weight_copies.append(pltpu.make_async_copy(w_down_ref, w_dn, local_sems.at[2 + 2 * local]))
+    weight_copies.insert(0, pltpu.make_async_copy(w_down_ref, w_dn, local_sems.at[2 + 2 * local]))
     for copy in row_copies + weight_copies:
         copy.start()
 
@@ -156,8 +156,7 @@
             x_rows = rows_buf[s, :, :, :, 0, :, cols].reshape(rows, k_tile)
             g_rows = rows_buf[s, :, :, :, 1, :, cols].reshape(rows, k_tile)
             acc_in[...] += jnp.dot(x_rows, w_cat[cols, :], preferred_element_type=F32)
-            down = w_dn[:, :, cols].reshape(local * hid, k_tile)
-            acc_hid[...] += lax.dot_general(g_rows, down, NT, preferred_element_type=F32)
+            acc_hid[...] += jnp.dot(g_rows, w_dn_t[cols, :], preferred_element_type=F32)
 
         tail = pl.ds(width, LANES)
         wts = rows_buf[s, :, :, :, 0, :, tail].reshape(rows, LANES).astype(F32)
@@ -174,8 +173,8 @@
             ).astype(BF16)
             hid_grads[:, (2 * e + 1) * hid : (2 * e + 2) * hid] = (grad * gate * sig).astype(BF16)
         for half in range(2):
-            w_rows = pl.ds(half * half_w, half_w)
-            value = lax.dot_general(hid_grads[...], w_cat[w_rows, :], NT, preferred_element_type=F32)
+            w_cols = pl.ds(half * half_w, half_w)
+            value = jnp.dot(hid_grads[...], w_cat_t[:, w_cols], preferred_element_type=F32)
             value = value.astype(BF16).reshape(2, 2, 2, toks, half_w)
             part[i, half, 0] = value[:, :, 0]
             part[i, half, 1] = value[:, :, 1]
@@ -217,14 +216,34 @@
             copy.start()
             z_sent.append((copy, None))
 
+    turn = 256
+
+    def turn_down(e):
+        @pl.loop(0, width // turn)
+        def _(j):
+            cols = pl.ds(pl.multiple_of(j * turn, turn), turn)
+            w_dn_t[cols, e * hid : (e + 1) * hid] = w_dn[e, :, cols].T
+
+    def turn_cat(e):
+        span = pl.ds(2 * e * hid, 2 * hid)
+
+        @pl.loop(0, width // turn)
+        def _(j):
+            cols = pl.ds(pl.multiple_of(j * turn, turn), turn)
+            w_cat_t[span, cols] = w_cat[cols, span].T
+
     to_plane(0)
+    for copy in weight_copies:
+        copy.wait()
+    for e in range(local):
+        turn_down(e)
     from_z(1)
     relay(0)
     from_z(2)
     relay(1)
+    for e in range(local):
+        turn_cat(e)
     share_diagonal(0)
-    for copy in weight_copies:
-        copy.wait()
     compute(0)
     from_z(3)
     relay(2)
@@ -277,6 +296,8 @@
         pltpu.VMEM((4, 2, 2, 2, 2, toks, width + LANES), BF16),
         pltpu.VMEM((width, 2 * local * hid), BF16),
         pltpu.VMEM((local, hid, width), BF16),
+        pltpu.VMEM((2 * local * hid, width), BF16),
+        pltpu.VMEM((width, local * hid), BF16),
         pltpu.VMEM((rows, 2 * local * hid), F32),
         pltpu.VMEM((rows, local * hid), F32),
         pltpu.VMEM((rows, 2 * local * hid), BF16),

time: 78.7 us -> 75 us (0.953)
  Pallas kernels: 77 us -> 73.2 us
    pallas_call x1, Pallas kernels: 77 us -> 73.2 us  [fused(): pl.pallas_call(fused_kernel, out_shape=jax.ShapeDtypeStruct((toks, width)...]
where the time goes in v4:
time: 75 us; the launch traced here: 74.8 us
  Pallas kernels  73.2 us (98%)
  local copies, waits for them, and re-layouts  1.55 us (2%)
    pallas_call x1, Pallas kernels, fused(): pl.pallas_call(fused_kernel, out_shape=jax.ShapeDtypeStruct((toks, width)...  73.2 us
    unnamed x1, local copies, waits for them, and re-layouts  1.55 us

profile of v4, /device:TPU:0, one launch (start us, length us, event | category | flops | bytes accessed | tf_op | source)
XLA Modules:
  0.0 74.8 jit_solution(10477130183365590189)
XLA Ops:
  0.0 73.2 %shard_map.73 = bf16[16,3584]{1,0:T(8,128)(2,1)} custom-call(bf16[16,3584]{1,0:T(8,128)(2,1)} %tokens_ref.1, bf16[16,3584]{1,0:T(8,128)(2,1)} %grads_ref.1, s32[8,16]{1,0:T(8,128)} %bitcast.2, f32[8,16]{1,0:T(8,128)} %bitcast.3, bf16[2,3584,256]{2,1,0:T(8,128)(2,1)} %w_gate_ref.1, bf16[2,3584,256]{2,1,0:T(8,128)(2,1)} %w_up_ref.1, ...), custom_call_target="tpu_custom_call" | custom-call | flops 9395240960 | bytes 11010048 | tf_op jit(solution)/shard_map/pallas_call | solution.py:321
  73.2 1.6 %copy.9 = bf16[16,3584]{1,0:T(8,128)(2,1)} copy(bf16[16,3584]{1,0:T(8,128)(2,1)} %shard_map.73) | data formatting | bytes 229376

commit v5 on v4

--- a/solution.py
+++ b/solution.py
@@ -124,15 +124,20 @@
         along_z(s, z + 2 * up - 1, i)
         to_plane(i)
 
-    def relay(i):
-        x_in[i].wait_recv()
-        got = rows_buf.at[order[i], y, ox, c]
-        first = send(got.at[0], got.at[0], to_y)
-        core_in[i].append(send(got, got, to_core))
-        y_in[i].wait_recv()
-        got = rows_buf.at[order[i], oy, x, c]
-        diag_in[i] = (first, send(got.at[1], got.at[1], to_x))
-        core_in[i].append(send(got, got, to_core))
+    def relay(i, parts=("core", "diagonal")):
+        got_x = rows_buf.at[order[i], y, ox, c]
+        got_y = rows_buf.at[order[i], oy, x, c]
+        if parts[0] == "core":
+            x_in[i].wait_recv()
+        if "diagonal" in parts:
+            first = send(got_x.at[0], got_x.at[0], to_y)
+        if parts[0] == "core":
+            core_in[i].append(send(got_x, got_x, to_core))
+            y_in[i].wait_recv()
+        if "diagonal" in parts:
+            diag_in[i] = (first, send(got_y.at[1], got_y.at[1], to_x))
+        if parts[0] == "core":
+            core_in[i].append(send(got_y, got_y, to_core))
 
     def share_diagonal(i):
         for n in range(2):
@@ -143,7 +148,7 @@
     rows = 8 * toks
     k_tile = width // 2
 
-    def compute(i):
+    def compute(i, between):
         for copy in core_in[i]:
             copy.wait_recv()
         s = order[i]
@@ -172,6 +177,7 @@
                 grad * up * sig * (1.0 + gate * (1.0 - sig))
             ).astype(BF16)
             hid_grads[:, (2 * e + 1) * hid : (2 * e + 2) * hid] = (grad * gate * sig).astype(BF16)
+        between()
         for half in range(2):
             w_cols = pl.ds(half * half_w, half_w)
             value = jnp.dot(hid_grads[...], w_cat_t[:, w_cols], preferred_element_type=F32)
@@ -238,34 +244,31 @@
     for e in range(local):
         turn_down(e)
     from_z(1)
-    relay(0)
+    relay(0, ("core",))
     from_z(2)
     relay(1)
     for e in range(local):
         turn_cat(e)
+    share_diagonal(1)
+    compute(1, lambda: from_z(3))
+    relay(2)
+    reduce1(1)
+    share_diagonal(2)
+    compute(2, lambda: reduce2(1))
+    relay(3)
+    relay(0, ("diagonal",))
+    reduce1(2)
+    reduce3(1)
+    share_diagonal(3)
+    compute(3, lambda: reduce2(2))
     share_diagonal(0)
-    compute(0)
-    from_z(3)
-    relay(2)
-    share_diagonal(1)
+    reduce1(3)
+    reduce3(2)
+    compute(0, lambda: reduce2(3))
+    reduce3(3)
     reduce1(0)
-    compute(1)
-    relay(3)
-    share_diagonal(2)
-    reduce1(1)
     reduce2(0)
-    compute(2)
-    share_diagonal(3)
-    reduce1(2)
-    reduce2(1)
     reduce3(0)
-    compute(3)
-    reduce1(3)
-    reduce2(2)
-    reduce3(1)
-    reduce2(3)
-    reduce3(2)
-    reduce3(3)
     for s in order[1:]:
         got = z_got.at[s]
         z_copy(got, got, s, s, 1, 0).wait_recv()

time: 75 us -> 82.5 us (1.10)
  Pallas kernels: 73.2 us -> 80.7 us
    pallas_call x1, Pallas kernels: 73.2 us -> 80.7 us  [fused(): pl.pallas_call(fused_kernel, out_shape=jax.ShapeDtypeStruct((toks, width)...]
where the time goes in v5:
time: 82.5 us; the launch traced here: 82.2 us
  Pallas kernels  80.7 us (98%)
  local copies, waits for them, and re-layouts  1.55 us (2%)
    pallas_call x1, Pallas kernels, fused(): pl.pallas_call(fused_kernel, out_shape=jax.ShapeDtypeStruct((toks, width)...  80.7 us

profile of v5, /device:TPU:0, one launch (start us, length us, event | category | flops | bytes accessed | tf_op | source)
XLA Modules:
  0.0 82.2 jit_solution(8765209528438359159)
XLA Ops:
  0.0 80.7 %shard_map.73 = bf16[16,3584]{1,0:T(8,128)(2,1)} custom-call(bf16[16,3584]{1,0:T(8,128)(2,1)} %tokens_ref.1, bf16[16,3584]{1,0:T(8,128)(2,1)} %grads_ref.1, s32[8,16]{1,0:T(8,128)} %bitcast.2, f32[8,16]{1,0:T(8,128)} %bitcast.3, bf16[2,3584,256]{2,1,0:T(8,128)(2,1)} %w_gate_ref.1, bf16[2,3584,256]{2,1,0:T(8,128)(2,1)} %w_up_ref.1, ...), custom_call_target="tpu_custom_call" | custom-call | flops 9395240960 | bytes 11010048 | tf_op jit(solution)/shard_map/pallas_call | solution.py:324
  80.7 1.6 %copy.9 = bf16[16,3584]{1,0:T(8,128)(2,1)} copy(bf16[16,3584]{1,0:T(8,128)(2,1)} %shard_map.73) | data formatting | bytes 229376

commit v6 on v4

--- a/solution.py
+++ b/solution.py
@@ -143,7 +143,7 @@
     rows = 8 * toks
     k_tile = width // 2
 
-    def compute(i):
+    def compute(i, between=lambda: None):
         for copy in core_in[i]:
             copy.wait_recv()
         s = order[i]
@@ -172,6 +172,7 @@
                 grad * up * sig * (1.0 + gate * (1.0 - sig))
             ).astype(BF16)
             hid_grads[:, (2 * e + 1) * hid : (2 * e + 2) * hid] = (grad * gate * sig).astype(BF16)
+        between()
         for half in range(2):
             w_cols = pl.ds(half * half_w, half_w)
             value = jnp.dot(hid_grads[...], w_cat_t[:, w_cols], preferred_element_type=F32)
@@ -233,38 +234,37 @@
             w_cat_t[span, cols] = w_cat[cols, span].T
 
     to_plane(0)
-    for copy in weight_copies:
-        copy.wait()
+    weight_copies[0].wait()
     for e in range(local):
         turn_down(e)
     from_z(1)
     relay(0)
-    from_z(2)
-    relay(1)
+    for copy in weight_copies[1:]:
+        copy.wait()
     for e in range(local):
         turn_cat(e)
+    from_z(2)
     share_diagonal(0)
-    compute(0)
+    compute(0, lambda: relay(1))
     from_z(3)
+    reduce1(0)
     relay(2)
     share_diagonal(1)
-    reduce1(0)
     compute(1)
     relay(3)
-    share_diagonal(2)
     reduce1(1)
     reduce2(0)
+    share_diagonal(2)
     compute(2)
     share_diagonal(3)
     reduce1(2)
     reduce2(1)
     reduce3(0)
-    compute(3)
+    compute(3, lambda: reduce2(2))
+    reduce3(1)
     reduce1(3)
-    reduce2(2)
-    reduce3(1)
+    reduce3(2)
     reduce2(3)
-    reduce3(2)
     reduce3(3)
     for s in order[1:]:
         got = z_got.at[s]

time: 75 us -> 75.3 us (level)
  no operation moved by 1% of the time
where the time goes in v6:
time: 75.3 us; the launch traced here: 75.1 us
  Pallas kernels  73.5 us (98%)
  local copies, waits for them, and re-layouts  1.55 us (2%)
    pallas_call x1, Pallas kernels, fused(): pl.pallas_call(fused_kernel, out_shape=jax.ShapeDtypeStruct((toks, width)...  73.5 us
    unnamed x1, local copies, waits for them, and re-layouts  1.55 us

profile of v6, /device:TPU:0, one launch (start us, length us, event | category | flops | bytes accessed | tf_op | source)
XLA Modules:
  0.0 75.1 jit_solution(10687468138567065173)
XLA Ops:
  0.0 73.5 %shard_map.73 = bf16[16,3584]{1,0:T(8,128)(2,1)} custom-call(bf16[16,3584]{1,0:T(8,128)(2,1)} %tokens_ref.1, bf16[16,3584]{1,0:T(8,128)(2,1)} %grads_ref.1, s32[8,16]{1,0:T(8,128)} %bitcast.2, f32[8,16]{1,0:T(8,128)} %bitcast.3, bf16[2,3584,256]{2,1,0:T(8,128)(2,1)} %w_gate_ref.1, bf16[2,3584,256]{2,1,0:T(8,128)(2,1)} %w_up_ref.1, ...), custom_call_target="tpu_custom_call" | custom-call | flops 9395240960 | bytes 11010048 | tf_op jit(solution)/shard_map/pallas_call | solution.py:321
  73.5 1.6 %copy.9 = bf16[16,3584]{1,0:T(8,128)(2,1)} copy(bf16[16,3584]{1,0:T(8,128)(2,1)} %shard_map.73) | data formatting | bytes 229376
